TPU v7x, 256 devices: a whole 4x4x8 slice. The times are simulated.
256 devices in a mesh: dp: 2 (over z_hi), seq: 32 (over x, y, core), head: 4 (over z_lo).
Axes of the slice: x: 4, y: 4, z: 8 (z_hi: 2, z_lo: 4; z = z_hi * 4 + z_lo), core: 2. Of those that a mesh axis runs over, the one named last changes fastest.
Arguments:
- queries: bfloat16 [32768, 3584], P(('dp', 'seq', 'head')), may hold values from -30 to 30
- keys: bfloat16 [32768, 512], P(('dp', 'seq', 'head')), may hold values from -5 to 5
- values: bfloat16 [32768, 512], P(('dp', 'seq', 'head')), may hold values from -6 to 6
- doc_lengths: int32 [2, 3], replicated, may hold values from 1 to 8192, 16384 in all within a row
- block_order: int32 [128], replicated, may hold values from 0 to 127, each once
Outputs:
- attended: bfloat16 [32768, 3584], P(('dp', 'seq', 'head'))
Inputs may be any that keep to these rules, and one draw needn't show every extreme that they name: `doc_lengths`: each row sums to 16384, and its largest entry is exactly 8192. `block_order`: a permutation of the 128 global block numbers.
All inputs are finite; a program needn't handle non-finite values.
Results may differ from a plain program's by a relative error of at most 0.007.
Values may be sent and summed in bfloat16 or wider, within the bound.
No kernel may reach another device: no remote copies, remote signals or barrier semaphores. Data moves between devices by JAX's collectives and lax.ppermute only.
A program may use at most 64 MiB of HBM per device.

v0:
```python
import math

import jax
import jax.numpy as jnp
from jax import lax
from jax.sharding import PartitionSpec as P

HEAD_WIDTH = 128


def from_behind(block, axis, distance):
    devices = range(lax.axis_size(axis))
    route = [((i - distance) % len(devices), i) for i in devices]
    return lax.ppermute(block, axis, route)


def block_marks(block_order, doc_ends, block_index, block_rows, per_group):
    block_id = lax.dynamic_slice_in_dim(block_order, jnp.asarray(block_index), 1, 0)[0]
    seq_group = block_id // per_group
    positions = block_id % per_group * block_rows + jnp.arange(block_rows, dtype=jnp.int32)
    pick = (jnp.arange(doc_ends.shape[0], dtype=jnp.int32) == seq_group).astype(jnp.int32)
    limits = jnp.sum(pick[:, None] * doc_ends, axis=0)
    document = jnp.sum((positions[:, None] >= limits[None, :]).astype(jnp.int32), axis=1)
    return (seq_group * doc_ends.shape[1] + document, positions)


def body(queries, keys, values, doc_lengths, block_order):
    head_count = lax.axis_size("head")
    tok_rows = queries.shape[0]
    q_parts = queries.reshape(tok_rows, head_count, -1)
    kv_parts = jnp.concatenate(
        [keys.reshape(tok_rows, head_count, -1), values.reshape(tok_rows, head_count, -1)], axis=2
    )
    q_here, kv_here = (
        lax.all_to_all(q_parts, "head", split_axis=1, concat_axis=0, tiled=True),
        lax.all_to_all(kv_parts, "head", split_axis=1, concat_axis=0, tiled=True),
    )
    tile_rows = q_here.shape[0]
    block_rows = tile_rows // 2
    q_heads = q_parts.shape[2] // HEAD_WIDTH
    kv_heads = kv_parts.shape[2] // (2 * HEAD_WIDTH)
    query_group_width = q_heads // kv_heads
    q_blocks = q_here.reshape(2, block_rows, kv_heads, query_group_width, HEAD_WIDTH)
    kv_start = kv_here.reshape(tile_rows, 2 * kv_heads * HEAD_WIDTH)
    cycle_size = lax.axis_size(("dp", "seq"))
    position = lax.axis_index(("dp", "seq"))
    per_group = block_order.shape[0] // doc_lengths.shape[0]
    doc_ends = jnp.cumsum(doc_lengths, axis=1)
    q_marks = [
        block_marks(block_order, doc_ends, 2 * position + which, block_rows, per_group)
        for which in range(2)
    ]
    scale = 1.0 / math.sqrt(HEAD_WIDTH)

    def absorb_block(states, kv_block, k_index):
        k_labels, k_spots = block_marks(block_order, doc_ends, k_index, block_rows, per_group)
        key_block = kv_block[:, : kv_heads * HEAD_WIDTH].reshape(block_rows, kv_heads, HEAD_WIDTH)
        value_block = kv_block[:, kv_heads * HEAD_WIDTH :].reshape(block_rows, kv_heads, HEAD_WIDTH)
        updated = []
        for which in range(2):
            q_labels, q_spots = q_marks[which]
            query_block = q_blocks[which]
            allowed = (q_labels[:, None] == k_labels[None, :]) & (
                k_spots[None, :] <= q_spots[:, None]
            )

            def attend(current):
                run_max, totals, sums = current
                scores = (
                    jnp.einsum(
                        "qhgd,khd->hgqk", query_block, key_block, preferred_element_type=jnp.float32
                    )
                    * scale
                )
                scores = jnp.where(allowed[None, None], scores, -jnp.inf)
                new_max = jnp.maximum(run_max, jnp.max(scores, axis=-1))
                weights = jnp.exp(scores - new_max[..., None])
                fade = jnp.exp(run_max - new_max)
                totals = totals * fade + jnp.sum(weights, axis=-1)
                update = jnp.einsum(
                    "hgqk,khd->qhgd",
                    weights.astype(jnp.bfloat16),
                    value_block,
                    preferred_element_type=jnp.float32,
                )
                sums = sums * jnp.transpose(fade, (2, 0, 1))[..., None] + update
                return (new_max, totals, sums)

            def unchanged(current):
                return current

            updated.append(lax.cond(jnp.any(allowed), attend, unchanged, states[which]))
        return tuple(updated)

    def absorb_tile(states, kv_tile, block_owner):
        for which in range(2):
            states = absorb_block(
                states,
                kv_tile[which * block_rows : (which + 1) * block_rows],
                2 * block_owner + which,
            )
        return states

    empty_state = (
        jnp.full((kv_heads, query_group_width, block_rows), -1e30, jnp.float32),
        jnp.zeros((kv_heads, query_group_width, block_rows), jnp.float32),
        jnp.zeros((block_rows, kv_heads, query_group_width, HEAD_WIDTH), jnp.float32),
    )
    carried = (empty_state, empty_state)
    carried = absorb_tile(carried, kv_start, position)

    def advance(circuit, loop_state):
        current, moving = loop_state
        moving = from_behind(moving, ("dp", "seq"), 1)
        current = absorb_tile(current, moving, (position - circuit) % cycle_size)
        return (current, moving)

    carried, moving = lax.fori_loop(1, cycle_size, advance, (carried, kv_start))
    pieces = []
    for which in range(2):
        run_max, totals, sums = carried[which]
        pieces.append(sums / jnp.transpose(totals, (2, 0, 1))[..., None])
    attention_output = jnp.concatenate(pieces, axis=0)
    attention_output = attention_output.astype(jnp.bfloat16).reshape(
        tile_rows, 1, q_heads * HEAD_WIDTH
    )
    homed = lax.all_to_all(attention_output, "head", split_axis=0, concat_axis=1, tiled=True)
    return homed.reshape(tok_rows, head_count * q_heads * HEAD_WIDTH)


def solution(mesh):
    in_specs = (
        P(("dp", "seq", "head"), None),
        P(("dp", "seq", "head"), None),
        P(("dp", "seq", "head"), None),
        P(),
        P(),
    )
    out_specs = P(("dp", "seq", "head"), None)
    return jax.shard_map(body, mesh=mesh, in_specs=in_specs, out_specs=out_specs, check_vma=False)
```

profile of v0, /device:TPU:159, one launch (start us, length us, event | category | flops | bytes accessed | tf_op | source)
XLA Modules:
  0.0 1252.8 jit_solution(12226306067991225771)
XLA Ops:
  26.9 15.8 %all-to-all-done.1 = bf16[128,4,896]{0,2,1:T(8,128)(2,1)S(1)} async-done(((bf16[128,4,896]{0,2,1:T(8,128)(2,1)}), bf16[128,4,896]{0,2,1:T(8,128)(2,1)S(1)}, u32[]{:S(2)}, u32[]{:S(2)}) %all-to-all-start.1) | async-done | bytes 917536 | tf_op jit(solution)/shard_map/all_to_all | solution.py:35
  55.5 1159.1 %while.29 = (s32[]{:T(128)}, f32[1,7,256]{2,1,0:T(8,128)}, f32[1,7,256]{2,1,0:T(8,128)S(1)}, f32[256,1,7,128]{3,0,2,1:T(8,128)S(1)}, f32[1,7,256]{2,1,0:T(8,128)...) while((s32[]{:T(128)}, f32[1,7,256]{2,1,0:T(8,128)}, ...), condition=%wide.region_50.51_spmd.clone, body=%wide.region_25.50_spmd.clone.sunk | while | flops 955279936 | bytes 36667076 | solution.py:118
  69.2 8.8 collective-permute-start
  114.6 5.2 collective-permute-start
  153.0 5.9 collective-permute-start
  186.7 5.9 collective-permute-start
  223.9 5.9 collective-permute-start
  242.4 6.7 collective-permute-start
  311.8 5.9 collective-permute-start
  330.4 10.2 collective-permute-start
  507.8 5.2 collective-permute-start
  546.5 5.9 collective-permute-start
  596.0 7.6 collective-permute-start
  649.5 8.8 collective-permute-start
  671.1 6.7 collective-permute-start
  780.0 5.9 collective-permute-start
  798.5 5.9 collective-permute-start
  879.8 8.7 collective-permute-start
  938.8 8.8 collective-permute-start
  977.3 5.9 collective-permute-start
  1126.6 5.9 collective-permute-start
  1161.5 5.9 collective-permute-start
  1195.2 6.7 collective-permute-start
  1218.2 31.7 %all_to_all.45 = bf16[4,2,57344]{2,1,0:T(2,128)(2,1)S(1)} all-to-all(bf16[4,2,57344]{2,1,0:T(2,128)(2,1)S(1)} %reshape.542), channel_id=1, replica_groups=mesh['dp'=2,'seq'=32,'head'=4] {'head'}, dimensions={0} | all-to-all | bytes 1835008 | tf_op jit(solution)/shard_map/all_to_all | solution.py:127
  (2059 shorter events, 701.7 us)
Async XLA Ops:
  15.8 26.9 %all-to-all-start.1 = ((bf16[128,4,896]{0,2,1:T(8,128)(2,1)}), bf16[128,4,896]{0,2,1:T(8,128)(2,1)S(1)}, u32[]{:S(2)}, u32[]{:S(2)}) async-start(bf16[128,4,896]{0,2,1:T(8,128)(2,1)} %bitcast.132), calls=%async_computation.1 | async-start | bytes 1835008 | tf_op jit(solution)/shard_map/all_to_all | solution.py:35
  69.2 20.5 %collective-permute-start = (bf16[512,256]{1,0:T(8,128)(2,1)}, bf16[512,256]{1,0:T(8,128)(2,1)S(1)}, u32[]{:S(2)}, u32[]{:S(2)}) collective-permute-start(bf16[512,256]{1,0:T(8,128)(2,1)} %get-tuple-element.1264), channel_id=1, source_target_pairs={{252,0},{0,4},{4,8},{8,12},{12,16},{16,20},{20,24},{24,28},{28,32}... | collective-permute-start | bytes 786440 | tf_op jit(solution)/shard_map/while/body/eval_jaxpr/ppermute | solution.py:14
  114.6 16.9 %collective-permute-start = (bf16[512,256]{1,0:T(8,128)(2,1)}, bf16[512,256]{1,0:T(8,128)(2,1)S(1)}, u32[]{:S(2)}, u32[]{:S(2)}) collective-permute-start(bf16[512,256]{1,0:T(8,128)(2,1)} %get-tuple-element.1264), channel_id=1, source_target_pairs={{252,0},{0,4},{4,8},{8,12},{12,16},{16,20},{20,24},{24,28},{28,32}... | collective-permute-start | bytes 786440 | tf_op jit(solution)/shard_map/while/body/eval_jaxpr/ppermute | solution.py:14
  153.0 17.6 %collective-permute-start = (bf16[512,256]{1,0:T(8,128)(2,1)}, bf16[512,256]{1,0:T(8,128)(2,1)S(1)}, u32[]{:S(2)}, u32[]{:S(2)}) collective-permute-start(bf16[512,256]{1,0:T(8,128)(2,1)} %get-tuple-element.1264), channel_id=1, source_target_pairs={{252,0},{0,4},{4,8},{8,12},{12,16},{16,20},{20,24},{24,28},{28,32}... | collective-permute-start | bytes 786440 | tf_op jit(solution)/shard_map/while/body/eval_jaxpr/ppermute | solution.py:14
  186.7 17.6 %collective-permute-start = (bf16[512,256]{1,0:T(8,128)(2,1)}, bf16[512,256]{1,0:T(8,128)(2,1)S(1)}, u32[]{:S(2)}, u32[]{:S(2)}) collective-permute-start(bf16[512,256]{1,0:T(8,128)(2,1)} %get-tuple-element.1264), channel_id=1, source_target_pairs={{252,0},{0,4},{4,8},{8,12},{12,16},{16,20},{20,24},{24,28},{28,32}... | collective-permute-start | bytes 786440 | tf_op jit(solution)/shard_map/while/body/eval_jaxpr/ppermute | solution.py:14
  223.9 17.6 %collective-permute-start = (bf16[512,256]{1,0:T(8,128)(2,1)}, bf16[512,256]{1,0:T(8,128)(2,1)S(1)}, u32[]{:S(2)}, u32[]{:S(2)}) collective-permute-start(bf16[512,256]{1,0:T(8,128)(2,1)} %get-tuple-element.1264), channel_id=1, source_target_pairs={{252,0},{0,4},{4,8},{8,12},{12,16},{16,20},{20,24},{24,28},{28,32}... | collective-permute-start | bytes 786440 | tf_op jit(solution)/shard_map/while/body/eval_jaxpr/ppermute | solution.py:14
  242.4 18.4 %collective-permute-start = (bf16[512,256]{1,0:T(8,128)(2,1)}, bf16[512,256]{1,0:T(8,128)(2,1)S(1)}, u32[]{:S(2)}, u32[]{:S(2)}) collective-permute-start(bf16[512,256]{1,0:T(8,128)(2,1)} %get-tuple-element.1264), channel_id=1, source_target_pairs={{252,0},{0,4},{4,8},{8,12},{12,16},{16,20},{20,24},{24,28},{28,32}... | collective-permute-start | bytes 786440 | tf_op jit(solution)/shard_map/while/body/eval_jaxpr/ppermute | solution.py:14
  311.8 17.7 %collective-permute-start = (bf16[512,256]{1,0:T(8,128)(2,1)}, bf16[512,256]{1,0:T(8,128)(2,1)S(1)}, u32[]{:S(2)}, u32[]{:S(2)}) collective-permute-start(bf16[512,256]{1,0:T(8,128)(2,1)} %get-tuple-element.1264), channel_id=1, source_target_pairs={{252,0},{0,4},{4,8},{8,12},{12,16},{16,20},{20,24},{24,28},{28,32}... | collective-permute-start | bytes 786440 | tf_op jit(solution)/shard_map/while/body/eval_jaxpr/ppermute | solution.py:14
  330.4 22.0 %collective-permute-start = (bf16[512,256]{1,0:T(8,128)(2,1)}, bf16[512,256]{1,0:T(8,128)(2,1)S(1)}, u32[]{:S(2)}, u32[]{:S(2)}) collective-permute-start(bf16[512,256]{1,0:T(8,128)(2,1)} %get-tuple-element.1264), channel_id=1, source_target_pairs={{252,0},{0,4},{4,8},{8,12},{12,16},{16,20},{20,24},{24,28},{28,32}... | collective-permute-start | bytes 786440 | tf_op jit(solution)/shard_map/while/body/eval_jaxpr/ppermute | solution.py:14
  452.7 16.9 %collective-permute-start = (bf16[512,256]{1,0:T(8,128)(2,1)}, bf16[512,256]{1,0:T(8,128)(2,1)S(1)}, u32[]{:S(2)}, u32[]{:S(2)}) collective-permute-start(bf16[512,256]{1,0:T(8,128)(2,1)} %get-tuple-element.1264), channel_id=1, source_target_pairs={{252,0},{0,4},{4,8},{8,12},{12,16},{16,20},{20,24},{24,28},{28,32}... | collective-permute-start | bytes 786440 | tf_op jit(solution)/shard_map/while/body/eval_jaxpr/ppermute | solution.py:14
  507.8 17.0 %collective-permute-start = (bf16[512,256]{1,0:T(8,128)(2,1)}, bf16[512,256]{1,0:T(8,128)(2,1)S(1)}, u32[]{:S(2)}, u32[]{:S(2)}) collective-permute-start(bf16[512,256]{1,0:T(8,128)(2,1)} %get-tuple-element.1264), channel_id=1, source_target_pairs={{252,0},{0,4},{4,8},{8,12},{12,16},{16,20},{20,24},{24,28},{28,32}... | collective-permute-start | bytes 786440 | tf_op jit(solution)/shard_map/while/body/eval_jaxpr/ppermute | solution.py:14
  546.5 17.6 %collective-permute-start = (bf16[512,256]{1,0:T(8,128)(2,1)}, bf16[512,256]{1,0:T(8,128)(2,1)S(1)}, u32[]{:S(2)}, u32[]{:S(2)}) collective-permute-start(bf16[512,256]{1,0:T(8,128)(2,1)} %get-tuple-element.1264), channel_id=1, source_target_pairs={{252,0},{0,4},{4,8},{8,12},{12,16},{16,20},{20,24},{24,28},{28,32}... | collective-permute-start | bytes 786440 | tf_op jit(solution)/shard_map/while/body/eval_jaxpr/ppermute | solution.py:14
  596.0 19.3 %collective-permute-start = (bf16[512,256]{1,0:T(8,128)(2,1)}, bf16[512,256]{1,0:T(8,128)(2,1)S(1)}, u32[]{:S(2)}, u32[]{:S(2)}) collective-permute-start(bf16[512,256]{1,0:T(8,128)(2,1)} %get-tuple-element.1264), channel_id=1, source_target_pairs={{252,0},{0,4},{4,8},{8,12},{12,16},{16,20},{20,24},{24,28},{28,32}... | collective-permute-start | bytes 786440 | tf_op jit(solution)/shard_map/while/body/eval_jaxpr/ppermute | solution.py:14
  649.5 20.6 %collective-permute-start = (bf16[512,256]{1,0:T(8,128)(2,1)}, bf16[512,256]{1,0:T(8,128)(2,1)S(1)}, u32[]{:S(2)}, u32[]{:S(2)}) collective-permute-start(bf16[512,256]{1,0:T(8,128)(2,1)} %get-tuple-element.1264), channel_id=1, source_target_pairs={{252,0},{0,4},{4,8},{8,12},{12,16},{16,20},{20,24},{24,28},{28,32}... | collective-permute-start | bytes 786440 | tf_op jit(solution)/shard_map/while/body/eval_jaxpr/ppermute | solution.py:14
  671.1 18.5 %collective-permute-start = (bf16[512,256]{1,0:T(8,128)(2,1)}, bf16[512,256]{1,0:T(8,128)(2,1)S(1)}, u32[]{:S(2)}, u32[]{:S(2)}) collective-permute-start(bf16[512,256]{1,0:T(8,128)(2,1)} %get-tuple-element.1264), channel_id=1, source_target_pairs={{252,0},{0,4},{4,8},{8,12},{12,16},{16,20},{20,24},{24,28},{28,32}... | collective-permute-start | bytes 786440 | tf_op jit(solution)/shard_map/while/body/eval_jaxpr/ppermute | solution.py:14
  730.7 16.8 %collective-permute-start = (bf16[512,256]{1,0:T(8,128)(2,1)}, bf16[512,256]{1,0:T(8,128)(2,1)S(1)}, u32[]{:S(2)}, u32[]{:S(2)}) collective-permute-start(bf16[512,256]{1,0:T(8,128)(2,1)} %get-tuple-element.1264), channel_id=1, source_target_pairs={{252,0},{0,4},{4,8},{8,12},{12,16},{16,20},{20,24},{24,28},{28,32}... | collective-permute-start | bytes 786440 | tf_op jit(solution)/shard_map/while/body/eval_jaxpr/ppermute | solution.py:14
  780.0 17.6 %collective-permute-start = (bf16[512,256]{1,0:T(8,128)(2,1)}, bf16[512,256]{1,0:T(8,128)(2,1)S(1)}, u32[]{:S(2)}, u32[]{:S(2)}) collective-permute-start(bf16[512,256]{1,0:T(8,128)(2,1)} %get-tuple-element.1264), channel_id=1, source_target_pairs={{252,0},{0,4},{4,8},{8,12},{12,16},{16,20},{20,24},{24,28},{28,32}... | collective-permute-start | bytes 786440 | tf_op jit(solution)/shard_map/while/body/eval_jaxpr/ppermute | solution.py:14
  798.5 17.7 %collective-permute-start = (bf16[512,256]{1,0:T(8,128)(2,1)}, bf16[512,256]{1,0:T(8,128)(2,1)S(1)}, u32[]{:S(2)}, u32[]{:S(2)}) collective-permute-start(bf16[512,256]{1,0:T(8,128)(2,1)} %get-tuple-element.1264), channel_id=1, source_target_pairs={{252,0},{0,4},{4,8},{8,12},{12,16},{16,20},{20,24},{24,28},{28,32}... | collective-permute-start | bytes 786440 | tf_op jit(solution)/shard_map/while/body/eval_jaxpr/ppermute | solution.py:14
  879.8 20.5 %collective-permute-start = (bf16[512,256]{1,0:T(8,128)(2,1)}, bf16[512,256]{1,0:T(8,128)(2,1)S(1)}, u32[]{:S(2)}, u32[]{:S(2)}) collective-permute-start(bf16[512,256]{1,0:T(8,128)(2,1)} %get-tuple-element.1264), channel_id=1, source_target_pairs={{252,0},{0,4},{4,8},{8,12},{12,16},{16,20},{20,24},{24,28},{28,32}... | collective-permute-start | bytes 786440 | tf_op jit(solution)/shard_map/while/body/eval_jaxpr/ppermute | solution.py:14
  938.8 20.5 %collective-permute-start = (bf16[512,256]{1,0:T(8,128)(2,1)}, bf16[512,256]{1,0:T(8,128)(2,1)S(1)}, u32[]{:S(2)}, u32[]{:S(2)}) collective-permute-start(bf16[512,256]{1,0:T(8,128)(2,1)} %get-tuple-element.1264), channel_id=1, source_target_pairs={{252,0},{0,4},{4,8},{8,12},{12,16},{16,20},{20,24},{24,28},{28,32}... | collective-permute-start | bytes 786440 | tf_op jit(solution)/shard_map/while/body/eval_jaxpr/ppermute | solution.py:14
  977.3 17.6 %collective-permute-start = (bf16[512,256]{1,0:T(8,128)(2,1)}, bf16[512,256]{1,0:T(8,128)(2,1)S(1)}, u32[]{:S(2)}, u32[]{:S(2)}) collective-permute-start(bf16[512,256]{1,0:T(8,128)(2,1)} %get-tuple-element.1264), channel_id=1, source_target_pairs={{252,0},{0,4},{4,8},{8,12},{12,16},{16,20},{20,24},{24,28},{28,32}... | collective-permute-start | bytes 786440 | tf_op jit(solution)/shard_map/while/body/eval_jaxpr/ppermute | solution.py:14
  1126.6 17.7 %collective-permute-start = (bf16[512,256]{1,0:T(8,128)(2,1)}, bf16[512,256]{1,0:T(8,128)(2,1)S(1)}, u32[]{:S(2)}, u32[]{:S(2)}) collective-permute-start(bf16[512,256]{1,0:T(8,128)(2,1)} %get-tuple-element.1264), channel_id=1, source_target_pairs={{252,0},{0,4},{4,8},{8,12},{12,16},{16,20},{20,24},{24,28},{28,32}... | collective-permute-start | bytes 786440 | tf_op jit(solution)/shard_map/while/body/eval_jaxpr/ppermute | solution.py:14
  1161.5 17.6 %collective-permute-start = (bf16[512,256]{1,0:T(8,128)(2,1)}, bf16[512,256]{1,0:T(8,128)(2,1)S(1)}, u32[]{:S(2)}, u32[]{:S(2)}) collective-permute-start(bf16[512,256]{1,0:T(8,128)(2,1)} %get-tuple-element.1264), channel_id=1, source_target_pairs={{252,0},{0,4},{4,8},{8,12},{12,16},{16,20},{20,24},{24,28},{28,32}... | collective-permute-start | bytes 786440 | tf_op jit(solution)/shard_map/while/body/eval_jaxpr/ppermute | solution.py:14
  1195.2 18.4 %collective-permute-start = (bf16[512,256]{1,0:T(8,128)(2,1)}, bf16[512,256]{1,0:T(8,128)(2,1)S(1)}, u32[]{:S(2)}, u32[]{:S(2)}) collective-permute-start(bf16[512,256]{1,0:T(8,128)(2,1)} %get-tuple-element.1264), channel_id=1, source_target_pairs={{252,0},{0,4},{4,8},{8,12},{12,16},{16,20},{20,24},{24,28},{28,32}... | collective-permute-start | bytes 786440 | tf_op jit(solution)/shard_map/while/body/eval_jaxpr/ppermute | solution.py:14
  (307 other events, 892.8 us)
where the time goes:
time: 1270 us; the launch traced here: 1250 us
  loops' own time  510 us (40%)
  starting transfers between devices  224 us (18%)
  local copies, waits for them, and re-layouts  208 us (16%)
  other arithmetic  194 us (15%)
  matrix products  61 us (5%)
  blocking collectives  31.7 us (2%)
  waiting for transfers between devices  16 us (1%)
    another operation x1, loops' own time, body(): carried, moving = lax.fori_loop(1, cycle_size, advance, (carried, kv_start))  504 us
    ppermute x63, starting transfers between devices, from_behind(): return lax.ppermute(block, axis, route)  216 us
    reduce_or x63, other arithmetic, absorb_block(): updated.append(lax.cond(jnp.any(allowed), attend, unchanged, states[which]))  108 us
    squeeze x65, local copies, waits for them, and re-layouts, absorb_block(): query_block = q_blocks[which]  77.5 us
    while x567, local copies, waits for them, and re-layouts  44.7 us
    dynamic_slice x64, local copies, waits for them, and re-layouts, block_marks(): lax.dynamic_slice_in_dim(block_order, jnp.asarray(block_index), 1, 0)[0]  43.6 us
    all_to_all x1, blocking collectives, body(): lax.all_to_all(attention_output, 'head', split_axis=0, concat_axis=1, til...  31.7 us
    dot_general x40, matrix products, attend(): jnp.einsum('qhgd,khd->hgqk', query_block, key_block, preferred_element_ty...  31.1 us
  transfers between devices with their start and end apart: 65, of which 1 were waited for; matrix products, arithmetic and copies ran while one was open for 20% of the time, Pallas kernels for 0%

commit v1 on v0

v1 whole, which is shorter than its diff:
```python
import math

import jax
import jax.numpy as jnp
from jax import lax
from jax.experimental import pallas as pl
from jax.experimental.pallas import tpu as pltpu
from jax.sharding import PartitionSpec as P

HEAD_WIDTH = 128
ALL = ("dp", "seq", "head")
HEADS = 7
BLOCK = 256
SEQ_LEN = 16384
PER_SEQ = 64
MEMBERS = 32
STEP = 512
PAIRS = 4
SPAN = PAIRS * STEP
ROWS = 16
PAIR_ROWS = HEADS * ROWS
NEG = -1e30
SCALE = math.log2(math.e) / math.sqrt(HEAD_WIDTH)


def attend_tile(meta, q_ref, kv_ref, o_ref, stacked, peak, total):
    first = pl.program_id(0) * SPAN
    me = meta[2]
    ends = (meta[0], meta[1])
    for pair in range(PAIRS):
        for head in range(HEADS):
            at = pair * PAIR_ROWS + head * ROWS
            stacked[at : at + ROWS, :] = q_ref[
                pair * ROWS : (pair + 1) * ROWS, head * HEAD_WIDTH : (head + 1) * HEAD_WIDTH
            ]

    def start_of(position):
        return jnp.where(
            position >= ends[1], ends[1], jnp.where(position >= ends[0], ends[0], 0)
        )

    begin = start_of(first) // STEP
    diagonal = first // STEP
    clean = jnp.clip((start_of(first + SPAN - 1) + STEP - 1) // STEP, begin, diagonal)

    def spread(index):
        return (index // 8) * BLOCK + ((index // 4) % 2) * (BLOCK // 2) + index % 4

    row = lax.broadcasted_iota(jnp.int32, (PAIR_ROWS, 1), 0)
    column = lax.broadcasted_iota(jnp.int32, (1, STEP), 1)
    q_places = spread(row % ROWS) + 4 * me
    k_places = spread(column % ROWS) + 4 * (column // ROWS)
    peak[...] = jnp.full(peak.shape, NEG, jnp.float32)
    total[...] = jnp.zeros(total.shape, jnp.float32)
    ones = jnp.ones((STEP, HEAD_WIDTH), jnp.bfloat16)

    def absorb(step, from_pair, masked):
        block = kv_ref[:, pl.ds(pl.multiple_of(step * ROWS, ROWS), ROWS), :].reshape(
            STEP, 2 * HEAD_WIDTH
        )
        keys = block[:, :HEAD_WIDTH]
        values = jnp.concatenate([block[:, HEAD_WIDTH:], ones], axis=1)
        for pair in range(from_pair, PAIRS):
            rows = slice(pair * PAIR_ROWS, (pair + 1) * PAIR_ROWS)
            score = SCALE * lax.dot_general(
                stacked[rows, :], keys, (((1,), (1,)), ((), ())), preferred_element_type=jnp.float32
            )
            if masked:
                q_spots = q_places + (first + pair * STEP)
                k_spots = k_places + step * STEP
                seen = (k_spots >= start_of(q_spots)) & (k_spots <= q_spots)
                score = jnp.where(seen, score, NEG)
            before = peak[rows, :]
            now = jnp.maximum(before, jnp.max(score, axis=1, keepdims=True))
            peak[rows, :] = now
            fade = jnp.exp2(before - now)
            weight = jnp.exp2(score - jnp.concatenate([now] * (STEP // HEAD_WIDTH), axis=1))
            update = jnp.dot(
                weight.astype(jnp.bfloat16), values, preferred_element_type=jnp.float32
            )
            total[rows, :] = total[rows, :] * jnp.concatenate([fade] * 2, axis=1) + update

    @pl.loop(begin, clean)
    def _(step):
        absorb(step, 0, True)

    @pl.loop(clean, diagonal)
    def _(step):
        absorb(step, 0, False)

    for pair in range(PAIRS):
        absorb(diagonal + pair, pair, True)
    for pair in range(PAIRS):
        for head in range(HEADS):
            at = pair * PAIR_ROWS + head * ROWS
            mean = total[at : at + ROWS, :HEAD_WIDTH] / total[at : at + ROWS, HEAD_WIDTH:]
            o_ref[
                pair * ROWS : (pair + 1) * ROWS, head * HEAD_WIDTH : (head + 1) * HEAD_WIDTH
            ] = mean.astype(o_ref.dtype)


def attend(queries, keys_values, meta):
    rows, width = queries.shape
    tile_rows = PAIRS * ROWS
    return pl.pallas_call(
        attend_tile,
        out_shape=jax.ShapeDtypeStruct((rows, width), jnp.bfloat16),
        grid_spec=pltpu.PrefetchScalarGridSpec(
            num_scalar_prefetch=1,
            grid=(rows // tile_rows,),
            in_specs=[
                pl.BlockSpec((tile_rows, width), lambda i, m: (i, 0)),
                pl.BlockSpec(keys_values.shape, lambda i, m: (0, 0, 0)),
            ],
            out_specs=pl.BlockSpec((tile_rows, width), lambda i, m: (i, 0)),
            scratch_shapes=[
                pltpu.VMEM((PAIRS * PAIR_ROWS, HEAD_WIDTH), jnp.bfloat16),
                pltpu.VMEM((PAIRS * PAIR_ROWS, HEAD_WIDTH), jnp.float32),
                pltpu.VMEM((PAIRS * PAIR_ROWS, 2 * HEAD_WIDTH), jnp.float32),
            ],
        ),
        compiler_params=pltpu.CompilerParams(vmem_limit_bytes=48 * 1024 * 1024),
    )(meta, queries, keys_values)


def scatter_rows(rows):
    width = rows.shape[2]
    pieces = rows.reshape(MEMBERS, 4, 4, width).transpose(0, 2, 1, 3)
    both = jnp.broadcast_to(pieces[None], (2,) + pieces.shape).reshape(256, 4, width)
    return lax.all_to_all(both, ALL, split_axis=0, concat_axis=0, tiled=True)


def body(queries, keys, values, doc_lengths, block_order):
    tok_rows = queries.shape[0]
    sequence = lax.axis_index("dp")
    member = lax.axis_index("seq")
    place = lax.axis_index(ALL)
    ends = jnp.cumsum(doc_lengths, axis=1).astype(jnp.int32)
    my_ends = lax.dynamic_index_in_dim(ends, sequence, 0, keepdims=False)
    meta = jnp.stack([my_ends[0], my_ends[1], member]).astype(jnp.int32)

    source = jnp.arange(256 * 4, dtype=jnp.int32)
    target = jnp.arange(PER_SEQ * 8, dtype=jnp.int32)
    block_of_source = jnp.repeat(block_order, 8)
    slot_of_source = (block_of_source - sequence * PER_SEQ) * 8 + source % 8
    pick = (target[:, None] == slot_of_source[None, :]).astype(jnp.bfloat16)

    kv = jnp.concatenate(
        [keys.reshape(tok_rows, 4, HEAD_WIDTH), values.reshape(tok_rows, 4, HEAD_WIDTH)], axis=2
    )
    kv_got = scatter_rows(kv).reshape(1024, 2 * HEAD_WIDTH)
    kv_mine = jnp.dot(pick, kv_got, preferred_element_type=jnp.float32).astype(jnp.bfloat16)
    kv_all = lax.all_gather(kv_mine, "seq", axis=0, tiled=False)

    q_got = scatter_rows(queries.reshape(tok_rows, 4, HEADS * HEAD_WIDTH))
    q_got = q_got.reshape(1024, HEADS * HEAD_WIDTH)
    q_mine = jnp.dot(pick, q_got, preferred_element_type=jnp.float32).astype(jnp.bfloat16)

    out = attend(q_mine, kv_all, meta)

    back = lax.dot_general(
        pick, out, (((0,), (0,)), ((), ())), preferred_element_type=jnp.float32
    ).astype(jnp.bfloat16)
    home = lax.all_to_all(
        back.reshape(256, 4, HEADS * HEAD_WIDTH), ALL, split_axis=0, concat_axis=0, tiled=True
    )
    my_sequence = lax.dynamic_slice_in_dim(block_order, place // 2, 1, 0)[0] // PER_SEQ
    home = lax.dynamic_index_in_dim(
        home.reshape(2, MEMBERS, 4, 4, HEADS * HEAD_WIDTH), my_sequence, 0, keepdims=False
    )
    return home.transpose(0, 2, 1, 3).reshape(tok_rows, 4 * HEADS * HEAD_WIDTH)


def solution(mesh):
    rows = P(ALL, None)
    return jax.shard_map(
        body,
        mesh=mesh,
        in_specs=(rows, rows, rows, P(), P()),
        out_specs=rows,
        check_vma=False,
    )
```

time: 1270 us -> 233 us (0.18)
  the two profiles are of different devices: /device:TPU:159 before, /device:TPU:1 now
where the time goes in v1:
time: 233 us; the launch traced here: 231 us
  waiting for transfers between devices  114 us (49%)
  Pallas kernels  48.5 us (21%)
  starting transfers between devices  29.9 us (13%)
  between operations  16.2 us (7%)
  local copies, waits for them, and re-layouts  14.1 us (6%)
  matrix products  6.46 us (3%)
    all_to_all x2, waiting for transfers between devices, scatter_rows(): return lax.all_to_all(both, ALL, split_axis=0, concat_axis=0, tiled=True)  65.1 us
    pallas_call x1, Pallas kernels, attend(): pl.pallas_call(attend_tile, out_shape=jax.ShapeDtypeStruct((rows, width),...  48.5 us
    all_to_all x1, waiting for transfers between devices, body(): lax.all_to_all(back.reshape(256, 4, HEADS * HEAD_WIDTH), ALL, split_axis=...  44.1 us
    all_to_all x2, starting transfers between devices, scatter_rows(): return lax.all_to_all(both, ALL, split_axis=0, concat_axis=0, tiled=True)  22 us
    all_to_all x1, starting transfers between devices, body(): lax.all_to_all(back.reshape(256, 4, HEADS * HEAD_WIDTH), ALL, split_axis=...  7.87 us
    all_gather x1, waiting for transfers between devices, body(): kv_all = lax.all_gather(kv_mine, 'seq', axis=0, tiled=False)  5.05 us
  transfers between devices with their start and end apart: 4, of which 4 were waited for; matrix products, arithmetic and copies ran while one was open for 4% of the time, Pallas kernels for 0%

profile of v1, /device:TPU:1, one launch (start us, length us, event | category | flops | bytes accessed | tf_op | source)
XLA Modules:
  0.0 230.9 jit_solution(4671981119613450872)
XLA Ops:
  6.5 1.0 concatenate.8
  7.5 0.9 concatenate.9
  8.7 0.9 broadcast_in_dim.8
  9.6 15.7 %all-to-all-start.1 = ((bf16[256,4,256]{2,1,0:T(4,128)(2,1)}), bf16[256,4,256]{2,1,0:T(4,128)(2,1)S(1)}, u32[]{:S(2)}, u32[]{:S(2)}) async-start(bf16[256,4,256]{2,1,0:T(4,128)(2,1)} %bitcast.6), calls=%async_computation.1 | async-start | bytes 1048576 | tf_op jit(solution)/shard_map/all_to_all | solution.py:130
  25.6 19.7 %all-to-all-done.1 = bf16[256,4,256]{2,1,0:T(4,128)(2,1)S(1)} async-done(((bf16[256,4,256]{2,1,0:T(4,128)(2,1)}), bf16[256,4,256]{2,1,0:T(4,128)(2,1)S(1)}, u32[]{:S(2)}, u32[]{:S(2)}) %all-to-all-start.1) | async-done | bytes 524320 | tf_op jit(solution)/shard_map/all_to_all | solution.py:130
  45.4 1.2 fusion.5
  46.8 0.4 copy.9
  47.2 1.8 broadcast_in_dim.7
  48.9 6.3 %all-to-all-start = ((bf16[256,4,896]{2,1,0:T(4,128)(2,1)}), bf16[256,4,896]{2,1,0:T(4,128)(2,1)S(1)}, u32[]{:S(2)}, u32[]{:S(2)}) async-start(bf16[256,4,896]{2,1,0:T(4,128)(2,1)} %bitcast.21), calls=%async_computation | async-start | bytes 3670016 | tf_op jit(solution)/shard_map/all_to_all | solution.py:130
  55.5 0.6 fusion.13
  56.1 1.2 pad_add_fusion.meta
  57.3 45.4 %all-to-all-done = bf16[256,4,896]{2,1,0:T(4,128)(2,1)S(1)} async-done(((bf16[256,4,896]{2,1,0:T(4,128)(2,1)}), bf16[256,4,896]{2,1,0:T(4,128)(2,1)S(1)}, u32[]{:S(2)}, u32[]{:S(2)}) %all-to-all-start) | async-done | bytes 1835040 | tf_op jit(solution)/shard_map/all_to_all | solution.py:130
  102.7 1.5 reshape.54
  104.2 2.7 %fusion.4.q_ref = bf16[512,896]{1,0:T(8,128)(2,1)S(1)} fusion(bf16[1024,896]{1,0:T(8,128)(2,1)} %reshape.54, s32[1024]{0:T(1024)S(1)} %fusion.9), kind=kOutput, calls=%fused_computation.5 | convolution fusion | flops 940507136 | bytes 2756608 | tf_op jit(solution)/shard_map/dot_general | solution.py:157
  107.0 5.1 %all-gather.3.cloned.1.call-done = bf16[16384,256]{1,0:T(8,128)(2,1)} async-done(((bf16[512,256]{1,0:T(8,128)(2,1)}), bf16[16384,256]{1,0:T(8,128)(2,1)}) %all-gather.3.cloned.1.call-update) | async-done | bytes 8388624 | tf_op jit(solution)/shard_map/all_gather | solution.py:153
  112.0 48.5 %shard_map.55 = bf16[512,896]{1,0:T(8,128)(2,1)S(1)} custom-call(s32[3]{0:T(128)S(1)} %pad_add_fusion.meta, bf16[512,896]{1,0:T(8,128)(2,1)S(1)} %fusion.4.q_ref, bf16[32,512,256]{2,1,0:T(8,128)(2,1)} %bitcast.20), custom_call_target="tpu_custom_call" | custom-call | tf_op jit(solution)/shard_map/pallas_call | solution.py:105
  160.5 2.5 %fusion.3 = bf16[1024,896]{1,0:T(8,128)(2,1)} fusion(bf16[512,896]{1,0:T(8,128)(2,1)S(1)} %shard_map.55, s32[1024]{0:T(1024)S(1)} %fusion.9), kind=kOutput, calls=%fused_computation.4 | convolution fusion | flops 940965888 | bytes 2756608 | tf_op jit(solution)/shard_map/dot_general | solution.py:161
  163.1 4.1 %reshape.57 = bf16[256,4,896]{2,1,0:T(4,128)(2,1)} reshape(bf16[1024,896]{1,0:T(8,128)(2,1)} %fusion.3) | data formatting | bytes 3670016 | tf_op jit(solution)/shard_map/reshape | solution.py:165
  167.2 7.9 %all-to-all-start.2 = ((bf16[256,4,896]{2,1,0:T(4,128)(2,1)}), bf16[256,4,896]{2,1,0:T(4,128)(2,1)S(1)}, u32[]{:S(2)}, u32[]{:S(2)}) async-start(bf16[256,4,896]{2,1,0:T(4,128)(2,1)} %reshape.57), calls=%async_computation.2 | async-start | bytes 3670016 | tf_op jit(solution)/shard_map/all_to_all | solution.py:164
  175.1 0.6 dynamic_slice.12
  178.3 44.1 %all-to-all-done.2 = bf16[256,4,896]{2,1,0:T(4,128)(2,1)S(1)} async-done(((bf16[256,4,896]{2,1,0:T(4,128)(2,1)}), bf16[256,4,896]{2,1,0:T(4,128)(2,1)S(1)}, u32[]{:S(2)}, u32[]{:S(2)}) %all-to-all-start.2) | async-done | bytes 1835040 | tf_op jit(solution)/shard_map/all_to_all | solution.py:164
  222.4 0.3 constant_dynamic-slice_fusion
  222.7 0.4 copy.11
  223.1 1.0 copy.12
  (18 shorter events, 1.0 us)
Async XLA Ops:
  6.5 18.8 %copy-start.2 = (s32[128]{0:T(128)S(1)}, s32[128]{0:T(128)}, u32[]{:S(2)}) copy-start(s32[128]{0:T(128)} %param.9) | copy-start | bytes 1540
  9.6 35.6 %all-to-all-start.1 = ((bf16[256,4,256]{2,1,0:T(4,128)(2,1)}), bf16[256,4,256]{2,1,0:T(4,128)(2,1)S(1)}, u32[]{:S(2)}, u32[]{:S(2)}) async-start(bf16[256,4,256]{2,1,0:T(4,128)(2,1)} %bitcast.6), calls=%async_computation.1 | async-start | bytes 1048576 | tf_op jit(solution)/shard_map/all_to_all | solution.py:130
  25.3 21.3 %copy-start = (bf16[128,3584]{1,0:T(8,128)(2,1)S(1)}, bf16[128,3584]{1,0:T(8,128)(2,1)}, u32[]{:S(2)}) copy-start(bf16[128,3584]{1,0:T(8,128)(2,1)} %param.5) | copy-start | bytes 2752516
  25.3 86.7 %all-gather.3.cloned.1.call-start = ((), (), s32[]{:S(2)}) async-start(), calls=%async_computation.3 | async-start | bytes 8650752 | tf_op jit(solution)/shard_map/all_gather | solution.py:153
  48.9 6.3 %copy-start.1 = (s32[2,3]{1,0:T(2,128)S(1)}, s32[2,3]{1,0:T(2,128)}, u32[]{:S(2)}) copy-start(s32[2,3]{1,0:T(2,128)} %param.8) | copy-start | bytes 76
  48.9 53.8 %all-to-all-start = ((bf16[256,4,896]{2,1,0:T(4,128)(2,1)}), bf16[256,4,896]{2,1,0:T(4,128)(2,1)S(1)}, u32[]{:S(2)}, u32[]{:S(2)}) async-start(bf16[256,4,896]{2,1,0:T(4,128)(2,1)} %bitcast.21), calls=%async_computation | async-start | bytes 3670016 | tf_op jit(solution)/shard_map/all_to_all | solution.py:130
  167.2 55.2 %all-to-all-start.2 = ((bf16[256,4,896]{2,1,0:T(4,128)(2,1)}), bf16[256,4,896]{2,1,0:T(4,128)(2,1)S(1)}, u32[]{:S(2)}, u32[]{:S(2)}) async-start(bf16[256,4,896]{2,1,0:T(4,128)(2,1)} %reshape.57), calls=%async_computation.2 | async-start | bytes 3670016 | tf_op jit(solution)/shard_map/all_to_all | solution.py:164
Sparse Core Ops, SparseCore 0:
  46.7 65.2 all-gather.2
